TPU v7x, 128 devices: a whole 4x4x4 slice. The times are simulated.
128 devices in a mesh: op: 8 (over x, core), sec: 16 (over z, y).
Axes of the slice: x: 4, y: 4, z: 4, core: 2. Of those that a mesh axis runs over, the one named last changes fastest.
Arguments:
- psi: bfloat16 [32, 16, 256, 256], P('sec'), may hold values from -6 to 6
- left_ops: bfloat16 [64, 32, 256, 256], P('op', 'sec'), may hold values from -0.375 to 0.375
- right_ops: bfloat16 [64, 16, 256, 256], P('op', 'sec'), may hold values from -0.046875 to 0.046875
- left_size: int32 [32], replicated, may hold values from 1 to 256, 6144 in all
- right_size: int32 [16], replicated, may hold values from 1 to 256, 3072 in all
- left_charge: int32 [32], replicated, may hold values from 0 to 4
- right_charge: int32 [16], replicated, may hold values from 0 to 4
Outputs:
- sigma: bfloat16 [32, 16, 256, 256], P(None, 'sec', 'op')
Inputs may be any that keep to these rules, and one draw needn't show every extreme that they name: `left_size`: live rows of the left sectors sum to 6144. `right_size`: live columns of the right sectors sum to 3072.
All inputs are finite; a program needn't handle non-finite values.
Results may differ from a plain program's by a relative error of at most 0.0049.
Values may be sent and summed in bfloat16 or wider, within the bound.
A program may use at most 128 MiB of HBM per device.

v0:
```python
import jax
import jax.numpy as jnp
from jax import lax
from jax.sharding import PartitionSpec as P


def block_mask(start_left, count_left, left_size, right_size, left_charge, right_charge, blocks):
    left_q = lax.dynamic_slice_in_dim(left_charge, start_left, count_left, 0)
    left_live = lax.dynamic_slice_in_dim(left_size, start_left, count_left, 0)
    positions = jnp.arange(blocks, dtype=jnp.int32)
    allowed = jnp.abs(left_q[:, None] - right_charge[None, :]) <= 1
    rows = positions[None, :] < left_live[:, None]
    cols = positions[None, :] < right_size[:, None]
    return allowed[:, :, None, None] & rows[:, None, :, None] & cols[None, :, None, :]


def per_device(psi, left_ops, right_ops, left_size, right_size, left_charge, right_charge):
    left_count, right_all, blocks = (psi.shape[0], psi.shape[1], psi.shape[2])
    op_count = left_ops.shape[0]
    sector = lax.axis_index("sec")
    in_mask = block_mask(
        sector * left_count, left_count, left_size, right_size, left_charge, right_charge, blocks
    )
    masked = psi * in_mask.astype(jnp.bfloat16)
    piece = lax.all_gather(right_ops, "sec", axis=1, tiled=True)

    def one_term(index, accum):
        inner = jnp.einsum(
            "aij,abjl->abil", left_ops[index], masked, preferred_element_type=jnp.float32
        ).astype(jnp.bfloat16)
        return accum + jnp.einsum(
            "abil,bml->abim", inner, piece[index], preferred_element_type=jnp.float32
        )

    added = lax.fori_loop(0, op_count, one_term, jnp.zeros(masked.shape, jnp.float32))
    total = added
    total = jnp.where(in_mask, total, 0.0)
    banded = lax.psum_scatter(total, "op", scatter_dimension=2, tiled=True).astype(jnp.bfloat16)
    return lax.all_to_all(banded, "sec", split_axis=1, concat_axis=0, tiled=True)


def solution(mesh):
    in_specs = (
        P("sec", None, None, None),
        P("op", "sec", None, None),
        P("op", "sec", None, None),
        P(),
        P(),
        P(),
        P(),
    )
    out_specs = P(None, "sec", "op", None)
    return jax.shard_map(
        per_device, mesh=mesh, in_specs=in_specs, out_specs=out_specs, check_vma=False
    )
```

profile of v0, /device:TPU:32, one launch (start us, length us, event | category | flops | bytes accessed | tf_op | source)
XLA Modules:
  0.0 302.9 jit_solution(16444188639754963588)
XLA Ops:
  6.5 0.7 all-gather.2.cloned.1.call-update
  7.3 0.7 dynamic_slice.21
  8.1 0.7 dynamic_slice.20
  8.8 0.7 abs_compare_fusion
  9.5 0.7 iota_compare_fusion.1
  10.3 0.3 broadcast_and_fusion
  10.6 10.6 %and_select_fusion.1 = bf16[2,16,256,256]{3,1,0,2:T(8,128)(2,1)S(1)} fusion(bf16[2,16,256,256]{3,2,1,0:T(8,128)(2,1)} %param.9, pred[16,256]{1,0:T(8,128)(4,1)S(1)} %iota_compare_fusion.1, pred[2,16,256]{1,0,2:T(4,128)(4,1)S(1)} %broadcast_and_fusion), kind=kLoop, calls=%fused_computation.12 | loop fusion | flops 4194304 | bytes 8400896 | tf_op jit(solution)/shard_map/mul | solution.py:24
  21.2 4.4 %copy.12 = bf16[2,16,256,256]{3,2,1,0:T(8,128)(2,1)} copy(bf16[2,16,256,256]{3,1,0,2:T(8,128)(2,1)S(1)} %and_select_fusion.1) | data formatting | bytes 8388608
  25.6 97.2 %all-gather.2.cloned.1.call-done = bf16[8,16,256,256]{3,2,1,0:T(8,128)(2,1)} async-done(((bf16[8,1,256,256]{3,2,1,0:T(8,128)(2,1)}), bf16[8,16,256,256]{3,2,1,0:T(8,128)(2,1)}) %all-gather.2.cloned.1.call-update) | async-done | bytes 16777232 | tf_op jit(solution)/shard_map/all_gather | solution.py:25
  122.8 84.7 %while.14 = (s32[]{:T(128)}, f32[2,16,256,256]{2,3,0,1:T(8,128)}, bf16[8,16,256,256]{3,2,1,0:T(8,128)(2,1)}, bf16[8,2,256,256]{3,2,1,0:T(8,128)(2,1)}, bf16[2,16...) while((s32[]{:T(128)}, f32[2,16,256,256]{2,3,0,1:T(8,128)}, ...), condition=%wide.region_1.0_spmd.clone, body=%wide.region_0.0_spmd.clone.sunk | while | flops 2153775104 | bytes 23332444 | solution.py:35
  122.8 8.5 %bitcast_add_fusion.2 = f32[2,16,256,256]{2,3,0,1:T(8,128)} fusion(f32[2,16,256,256]{2,3,0,1:T(8,128)} %get-tuple-element.177, pred[]{:T(512)S(6)} %compare.3, bf16[2,16,256,256]{3,2,1,0:T(8,128)(2,1)} %get-tuple-element.187, bf16[8,16,256,256]{3,2,1,0:T(8,128)(2,1)} %get-tuple-element.185, s32[]{:T(128)S(6)} %copy.31, ...), kind=kOutput, calls=%fused_computation.clone.1 | convolution fusion | flops 2153775104 | bytes 23332352 | tf_op jit(solution)/shard_map/while/body/eval_jaxpr/abil,bml->abim/dot_general | solution.py:31
  131.3 10.9 %bitcast_add_fusion.2 = f32[2,16,256,256]{2,3,0,1:T(8,128)} fusion(f32[2,16,256,256]{2,3,0,1:T(8,128)} %get-tuple-element.177, pred[]{:T(512)S(6)} %compare.3, bf16[2,16,256,256]{3,2,1,0:T(8,128)(2,1)} %get-tuple-element.187, bf16[8,16,256,256]{3,2,1,0:T(8,128)(2,1)} %get-tuple-element.185, s32[]{:T(128)S(6)} %copy.31, ...), kind=kOutput, calls=%fused_computation.clone.1 | convolution fusion | flops 2153775104 | bytes 23332352 | tf_op jit(solution)/shard_map/while/body/eval_jaxpr/abil,bml->abim/dot_general | solution.py:31
  142.2 10.9 %bitcast_add_fusion.2 = f32[2,16,256,256]{2,3,0,1:T(8,128)} fusion(f32[2,16,256,256]{2,3,0,1:T(8,128)} %get-tuple-element.177, pred[]{:T(512)S(6)} %compare.3, bf16[2,16,256,256]{3,2,1,0:T(8,128)(2,1)} %get-tuple-element.187, bf16[8,16,256,256]{3,2,1,0:T(8,128)(2,1)} %get-tuple-element.185, s32[]{:T(128)S(6)} %copy.31, ...), kind=kOutput, calls=%fused_computation.clone.1 | convolution fusion | flops 2153775104 | bytes 23332352 | tf_op jit(solution)/shard_map/while/body/eval_jaxpr/abil,bml->abim/dot_general | solution.py:31
  153.1 10.9 %bitcast_add_fusion.2 = f32[2,16,256,256]{2,3,0,1:T(8,128)} fusion(f32[2,16,256,256]{2,3,0,1:T(8,128)} %get-tuple-element.177, pred[]{:T(512)S(6)} %compare.3, bf16[2,16,256,256]{3,2,1,0:T(8,128)(2,1)} %get-tuple-element.187, bf16[8,16,256,256]{3,2,1,0:T(8,128)(2,1)} %get-tuple-element.185, s32[]{:T(128)S(6)} %copy.31, ...), kind=kOutput, calls=%fused_computation.clone.1 | convolution fusion | flops 2153775104 | bytes 23332352 | tf_op jit(solution)/shard_map/while/body/eval_jaxpr/abil,bml->abim/dot_general | solution.py:31
  164.0 10.9 %bitcast_add_fusion.2 = f32[2,16,256,256]{2,3,0,1:T(8,128)} fusion(f32[2,16,256,256]{2,3,0,1:T(8,128)} %get-tuple-element.177, pred[]{:T(512)S(6)} %compare.3, bf16[2,16,256,256]{3,2,1,0:T(8,128)(2,1)} %get-tuple-element.187, bf16[8,16,256,256]{3,2,1,0:T(8,128)(2,1)} %get-tuple-element.185, s32[]{:T(128)S(6)} %copy.31, ...), kind=kOutput, calls=%fused_computation.clone.1 | convolution fusion | flops 2153775104 | bytes 23332352 | tf_op jit(solution)/shard_map/while/body/eval_jaxpr/abil,bml->abim/dot_general | solution.py:31
  174.9 10.9 %bitcast_add_fusion.2 = f32[2,16,256,256]{2,3,0,1:T(8,128)} fusion(f32[2,16,256,256]{2,3,0,1:T(8,128)} %get-tuple-element.177, pred[]{:T(512)S(6)} %compare.3, bf16[2,16,256,256]{3,2,1,0:T(8,128)(2,1)} %get-tuple-element.187, bf16[8,16,256,256]{3,2,1,0:T(8,128)(2,1)} %get-tuple-element.185, s32[]{:T(128)S(6)} %copy.31, ...), kind=kOutput, calls=%fused_computation.clone.1 | convolution fusion | flops 2153775104 | bytes 23332352 | tf_op jit(solution)/shard_map/while/body/eval_jaxpr/abil,bml->abim/dot_general | solution.py:31
  185.7 10.9 %bitcast_add_fusion.2 = f32[2,16,256,256]{2,3,0,1:T(8,128)} fusion(f32[2,16,256,256]{2,3,0,1:T(8,128)} %get-tuple-element.177, pred[]{:T(512)S(6)} %compare.3, bf16[2,16,256,256]{3,2,1,0:T(8,128)(2,1)} %get-tuple-element.187, bf16[8,16,256,256]{3,2,1,0:T(8,128)(2,1)} %get-tuple-element.185, s32[]{:T(128)S(6)} %copy.31, ...), kind=kOutput, calls=%fused_computation.clone.1 | convolution fusion | flops 2153775104 | bytes 23332352 | tf_op jit(solution)/shard_map/while/body/eval_jaxpr/abil,bml->abim/dot_general | solution.py:31
  196.6 10.9 %bitcast_add_fusion.2 = f32[2,16,256,256]{2,3,0,1:T(8,128)} fusion(f32[2,16,256,256]{2,3,0,1:T(8,128)} %get-tuple-element.177, pred[]{:T(512)S(6)} %compare.3, bf16[2,16,256,256]{3,2,1,0:T(8,128)(2,1)} %get-tuple-element.187, bf16[8,16,256,256]{3,2,1,0:T(8,128)(2,1)} %get-tuple-element.185, s32[]{:T(128)S(6)} %copy.31, ...), kind=kOutput, calls=%fused_computation.clone.1 | convolution fusion | flops 2153775104 | bytes 23332352 | tf_op jit(solution)/shard_map/while/body/eval_jaxpr/abil,bml->abim/dot_general | solution.py:31
  207.5 10.5 %copy.13 = f32[2,16,256,256]{3,1,0,2:T(8,128)} copy(f32[2,16,256,256]{2,3,0,1:T(8,128)} %get-tuple-element.99) | data formatting | bytes 16777216 | tf_op jit(solution)/shard_map/while | solution.py:35
  218.0 7.5 %and_select_fusion = f32[2,16,256,256]{3,1,0,2:T(8,128)} fusion(f32[2,16,256,256]{3,1,0,2:T(8,128)} %copy.13, pred[16,256]{1,0:T(8,128)(4,1)S(1)} %iota_compare_fusion.1, pred[2,16,256]{1,0,2:T(4,128)(4,1)S(1)} %broadcast_and_fusion), kind=kLoop, calls=%fused_computation.11 | loop fusion | flops 4194304 | bytes 16789504 | tf_op jit(solution)/shard_map/jit(_where)/select_n | solution.py:37
  225.5 52.3 %reduce-scatter.2.cloned.1.call-done = f32[2,16,32,256]{3,1,0,2:T(8,128)} async-done(((f32[2,16,256,256]{3,1,0,2:T(8,128)}), f32[2,16,32,256]{3,1,0,2:T(8,128)}) %reduce-scatter.2.cloned.1.call-update) | async-done | bytes 1048592 | tf_op jit(solution)/shard_map/reduce_scatter | solution.py:38
  277.9 1.3 convert_element_type.14
  279.5 15.8 %all_to_all.18 = bf16[2,16,32,256]{3,2,0,1:T(8,128)(2,1)S(1)} all-to-all(bf16[2,16,32,256]{3,2,0,1:T(8,128)(2,1)S(1)} %copy.14), channel_id=1, replica_groups=mesh['op'=8,'sec'=16] {'sec'}, dimensions={1} | all-to-all | bytes 1048576 | tf_op jit(solution)/shard_map/all_to_all | solution.py:39
  295.2 0.8 copy.36
  (6 shorter events, 0.4 us)
Async XLA Ops:
  6.5 116.3 %all-gather.2.cloned.1.call-start = ((), (), s32[]{:S(2)}) async-start(), calls=%async_computation.2 | async-start | bytes 17825792 | tf_op jit(solution)/shard_map/all_gather | solution.py:25
  7.3 270.6 %reduce-scatter.2.cloned.1.call-start = ((), (), s32[]{:S(2)}) async-start(), calls=%async_computation.3 | async-start | bytes 9437184 | tf_op jit(solution)/shard_map/reduce_scatter | solution.py:38
Sparse Core Ops, SparseCore 0:
  9.5 113.2 all-gather.1
  225.6 52.1 reduce-scatter.1
where the time goes:
time: 306 us; the launch traced here: 303 us
  waiting for transfers between devices  150 us (49%)
  matrix products  84.7 us (28%)
  other arithmetic  21.2 us (7%)
  local copies, waits for them, and re-layouts  17.4 us (6%)
  blocking collectives  15.8 us (5%)
  between operations  13.5 us (4%)
    all_gather x1, waiting for transfers between devices, per_device(): piece = lax.all_gather(right_ops, 'sec', axis=1, tiled=True)  97.2 us
    dot_general x8, matrix products, one_term(): jnp.einsum('abil,bml->abim', inner, piece[index], preferred_element_type=...  84.7 us
    reduce_scatter x1, waiting for transfers between devices, per_device(): lax.psum_scatter(total, 'op', scatter_dimension=2, tiled=True)  52.3 us
    all_to_all x1, blocking collectives, per_device(): lax.all_to_all(banded, 'sec', split_axis=1, concat_axis=0, tiled=True)  15.8 us
    mul x1, other arithmetic, per_device(): masked = psi * in_mask.astype(jnp.bfloat16)  10.6 us
    while x1, local copies, waits for them, and re-layouts, per_device(): lax.fori_loop(0, op_count, one_term, jnp.zeros(masked.shape, jnp.float32))  10.5 us
    select_n x1, other arithmetic, per_device(): total = jnp.where(in_mask, total, 0.0)  7.52 us
  transfers between devices with their start and end apart: 2, of which 2 were waited for; matrix products, arithmetic and copies ran while one was open for 6% of the time, Pallas kernels for 0%

commit v1 on v0

v1 whole, which is shorter than its diff:
```python
import jax
import jax.numpy as jnp
from jax import lax
from jax.experimental import pallas as pl
from jax.experimental.pallas import tpu as pltpu
from jax.sharding import PartitionSpec as P

MESH = pl.DeviceIdType.MESH
BLK = 256
NK = 8
ROWS = 64


def wrap(i):
    return lax.rem(i, 4)


def kernel(lsize, rsize, lcharge, rcharge, psi, left, right, out,
           lb, rb, pb, pm, inner, stage, far, from_left, from_right, fin, got,
           own_sem, p1_send, p1_recv, px_send, px_recv, r_send, r_recv, l_send, l_recv,
           x_send, far_recv, x_recv, f_send, f_recv):
    op, sec = lax.axis_index("op"), lax.axis_index("sec")
    x, c = lax.div(op, 2), lax.rem(op, 2)
    z, y = lax.div(sec, 4), lax.rem(sec, 4)
    p, q = y + c * (z - y), z + c * (y - z)

    def sec_at(pp, qq):
        return 4 * qq + pp + 3 * c * (pp - qq)

    def dev(dx=0, dp=0, dq=0, other=False):
        core = 1 - c if other else c
        return (2 * wrap(x + dx) + core, sec_at(wrap(p + dp), wrap(q + dq)))

    def remote(src, dst, send, recv, to):
        return pltpu.make_async_remote_copy(src_ref=src, dst_ref=dst, send_sem=send, recv_sem=recv, device_id=to, device_id_type=MESH)

    barrier = pltpu.get_barrier_semaphore()
    senders = [dev(dp=s) for s in (1, 2, 3)] + [dev(dq=s) for s in (1, 2, 3)] + [dev(dx=s) for s in (1, 3)]
    senders += [dev(dp=s, other=True) for s in range(4)]
    for to in senders:
        pl.semaphore_signal(barrier, 1, device_id=to, device_id_type=MESH)

    own = [pltpu.make_async_copy(psi.at[:, sec_at(p, wrap(q + r))], pb.at[r, pl.ds(0, 2)], own_sem.at[r]) for r in range(4)]
    own += [pltpu.make_async_copy(right.at[k, 0], rb.at[0, :, pl.ds(k * BLK, BLK)], own_sem.at[4 + k]) for k in range(NK)]
    band = [wrap(x + d) for d in (2, 1, 3, 0)]
    for j in range(4):
        rows = pl.ds(pl.multiple_of(band[j] * ROWS, ROWS), ROWS)
        own += [pltpu.make_async_copy(left.at[:, a, rows], lb.at[j, a], own_sem.at[12 + 2 * j + a]) for a in range(2)]
    for copy in own:
        copy.start()

    pl.semaphore_wait(barrier, len(senders))

    sent = []

    def start(copy):
        copy.start()
        sent.append(copy)

    p1 = {s: remote(psi.at[:, sec_at(wrap(p + s), wrap(q + x))], pb.at[x, pl.ds(2 * (4 - s), 2)], p1_send.at[s - 1], p1_recv.at[3 - s], dev(dp=s))
          for s in (1, 2, 3)}
    for s in (1, 3, 2):
        start(p1[s])

    def r_copy(k, to_right):
        return remote(right.at[k, 0], rb.at[3 if to_right else 1, :, pl.ds(k * BLK, BLK)],
                      r_send.at[0 if to_right else 1, k], r_recv.at[2 if to_right else 0, k], dev(dq=1 if to_right else 3))

    def r_pass(k):
        here = rb.at[3 if k < 4 else 1, :, pl.ds(k * BLK, BLK)]
        return remote(here, rb.at[2, :, pl.ds(k * BLK, BLK)], r_send.at[2, k], r_recv.at[1, k], dev(dq=1 if k < 4 else 3))

    for i in range(NK):
        start(r_copy(i, True))
        start(r_copy(NK - 1 - i, False))

    def l_copy(j, a, to_right):
        rows = pl.ds(pl.multiple_of(band[j] * ROWS, ROWS), ROWS)
        slot = 3 if to_right else 1
        return remote(left.at[:, a, rows], lb.at[j, 2 * slot + a], l_send.at[j, 0 if to_right else 1, a], l_recv.at[j, slot - 1, a], dev(dp=1 if to_right else 3))

    def l_pass(j, a):
        here = lb.at[j, 2 * (3 if a == 0 else 1) + a]
        return remote(here, lb.at[j, 4 + a], l_send.at[j, 2, a], l_recv.at[j, 1, a], dev(dp=1 if a == 0 else 3))

    def l_start(j):
        for i in range(2):
            start(l_copy(j, i, True))
            start(l_copy(j, 1 - i, False))

    def l_forward(j):
        for i in range(2):
            l_copy(j, i, True).wait_recv()
            if i == 0:
                start(l_pass(j, 0))
            l_copy(j, 1 - i, False).wait_recv()
            if i == 0:
                start(l_pass(j, 1))

    for s in (1, 3, 2):
        p1[s].wait_recv()

    def px_part(slot_x, i):
        return pb.at[wrap(x + slot_x), pl.ds(2, 6)] if i is None else px_view(slot_x, i)

    def px_view(slot_x, half):
        return pb.at[wrap(x + slot_x), pl.ds(2 + 3 * half, 3)]

    def px_copy(half, to_right):
        return remote(px_view(0, half), px_view(0, half), px_send.at[0 if to_right else 1, half], px_recv.at[2 if to_right else 0, half],
                      dev(dx=1 if to_right else 3))

    def px_pass(half):
        slot_x = 3 if half == 0 else 1
        return remote(px_view(slot_x, half), px_view(slot_x, half), px_send.at[2, half], px_recv.at[1, half], dev(dx=1 if half == 0 else 3))

    def px_arrive(slot_x, half):
        return remote(px_view(slot_x, half), px_view(slot_x, half), px_send.at[2, half], px_recv.at[slot_x - 1, half], dev(dx=1))

    for i in range(2):
        start(px_copy(i, True))
        start(px_copy(1 - i, False))

    for i in range(4):
        r_copy(i, True).wait_recv()
        start(r_pass(i))
        r_copy(NK - 1 - i, False).wait_recv()
        start(r_pass(NK - 1 - i))
    l_start(0)
    px_arrive(3, 0).wait_recv()
    start(px_pass(0))
    px_arrive(1, 1).wait_recv()
    start(px_pass(1))
    l_start(1)
    for i in range(4, NK):
        r_copy(i, True).wait_recv()
        r_copy(NK - 1 - i, False).wait_recv()
    for copy in own:
        copy.wait()
    l_forward(0)
    for k in range(NK):
        r_pass(k).wait_recv()
    px_arrive(3, 1).wait_recv()
    px_arrive(1, 0).wait_recv()
    px_arrive(2, 0).wait_recv()
    px_arrive(2, 1).wait_recv()

    row_at = lax.broadcasted_iota(jnp.int32, (BLK, BLK), 0)
    col_at = lax.broadcasted_iota(jnp.int32, (BLK, BLK), 1)

    def mask_block(n, _):
        r, sa = lax.div(n, 8), lax.rem(n, 8)
        a = 2 * sec_at(wrap(p + lax.div(sa, 2)), q) + lax.rem(sa, 2)
        b = sec_at(p, wrap(q + r))
        live = (row_at < lsize[a]) & (col_at < rsize[b])
        block = pb[r, sa].astype(jnp.float32)
        pm[r, sa] = jnp.where(live, block, 0.0).astype(jnp.bfloat16)
        return 0

    lax.fori_loop(0, 32, mask_block, 0)

    def product(j, r):
        def first(sa, _):
            lhs = lb[j, sa].reshape(NK * ROWS, BLK)
            part = jnp.dot(lhs, pm[r, sa], preferred_element_type=jnp.float32).astype(jnp.bfloat16)
            here = pl.ds(pl.multiple_of(sa * ROWS, ROWS), ROWS)
            for k in range(NK):
                inner[here, k * BLK:(k + 1) * BLK] = part[k * ROWS:(k + 1) * ROWS]
            return 0

        lax.fori_loop(0, 8, first, 0)
        return lax.dot_general(inner[...], rb[r], (((1,), (1,)), ((), ())), preferred_element_type=jnp.float32)

    def far_copy(r):
        return remote(stage.at[0, r], far.at[r], x_send.at[0, r], far_recv.at[r], dev(dx=1 + 2 * lax.div(r, 2)))

    def x_copy(side, r):
        return remote(stage.at[1 + side, r], (from_left, from_right)[side].at[r], x_send.at[1 + side, r], x_recv.at[side, r], dev(dx=(1, 3)[side]))

    def fin_copy(r, other):
        core = 1 - c if other else c
        return remote(fin.at[r, core], got.at[c, wrap(4 - r)], f_send.at[r, 1 if other else 0], f_recv.at[c, wrap(4 - r)], dev(dq=r, other=other))

    def stage_far(n, _):
        r = 2 * lax.rem(n, 2) + lax.div(n, 2)
        stage[0, r] = product(0, r).astype(jnp.bfloat16)
        far_copy(r).start()
        return 0

    def stage_side(side):
        def body(n, _):
            r = wrap(n + 2) if side == 0 else n
            total = product(1 + side, r)

            @pl.when(n < 2)
            def _():
                stage[1 + side, r] = total.astype(jnp.bfloat16)

            @pl.when(n >= 2)
            def _():
                far_copy(r).wait_recv()
                stage[1 + side, r] = (total + far[r].astype(jnp.float32)).astype(jnp.bfloat16)

            x_copy(side, r).start()
            return 0

        return body

    def stage_own(n, _):
        r = wrap(n + 1)
        total = product(3, r)
        x_copy(0, r).wait_recv()
        x_copy(1, r).wait_recv()
        total = total + from_left[r].astype(jnp.float32) + from_right[r].astype(jnp.float32)
        total = total.astype(jnp.bfloat16).reshape(8, ROWS, BLK)
        fin[r, 0] = total[:, :32]
        fin[r, 1] = total[:, 32:]
        fin_copy(r, True).start()

        @pl.when(n < 3)
        def _():
            fin_copy(r, False).start()

        return 0

    bodies = [stage_far, stage_side(0), stage_side(1), stage_own]
    for j in range(4):
        if j < 3:
            l_forward(j + 1)
            if j < 2:
                l_start(j + 2)
        l_pass(j, 0).wait_recv()
        l_pass(j, 1).wait_recv()
        lax.fori_loop(0, 4, bodies[j], 0)

    got[c, 0] = fin[0, c]

    def arrived(part, slot):
        return remote(fin.at[0, 0], got.at[part, slot], f_send.at[0, 0], f_recv.at[part, slot], dev(dq=1))

    for s in range(4):
        arrived(1 - c, s).wait_recv()
    for s in range(1, 4):
        arrived(c, s).wait_recv()

    row_at = lax.broadcasted_iota(jnp.int32, (32, BLK), 0) + 32 * op
    col_live = lax.broadcasted_iota(jnp.int32, (32, BLK), 1) < rsize[sec]

    def finish(n, _):
        sz, sy, i = lax.div(n, 8), lax.rem(lax.div(n, 2), 4), lax.rem(n, 2)
        a = 2 * (4 * wrap(z + sz) + wrap(y + sy)) + i
        total = got[0, sz, 2 * sy + i].astype(jnp.float32) + got[1, sy, 2 * sz + i].astype(jnp.float32)
        rows = jnp.where(jnp.abs(lcharge[a] - rcharge[sec]) <= 1, lsize[a], 0)
        out[a] = jnp.where((row_at < rows) & col_live, total, 0.0).astype(jnp.bfloat16)
        return 0

    lax.fori_loop(0, 32, finish, 0)

    for copy in sent:
        copy.wait_send()

    def drain(r, _):
        far_copy(r).wait_send()
        x_copy(0, r).wait_send()
        x_copy(1, r).wait_send()
        fin_copy(r, True).wait_send()
        return 0

    lax.fori_loop(0, 4, drain, 0)
    for r in range(1, 4):
        fin_copy(r, False).wait_send()


def per_device(psi, left_ops, right_ops, left_size, right_size, left_charge, right_charge):
    smem = pl.BlockSpec(memory_space=pltpu.SMEM)
    hbm = pl.BlockSpec(memory_space=pl.ANY)
    dma = pltpu.SemaphoreType.DMA
    band = (8, ROWS, BLK)
    result = pl.pallas_call(
        kernel,
        out_shape=jax.ShapeDtypeStruct((32, 32, BLK), jnp.bfloat16),
        in_specs=[smem] * 4 + [hbm] * 3,
        out_specs=pl.BlockSpec(memory_space=pltpu.VMEM),
        scratch_shapes=[
            pltpu.VMEM((4, 8, NK, ROWS, BLK), jnp.bfloat16),
            pltpu.VMEM((4, BLK, NK * BLK), jnp.bfloat16),
            pltpu.VMEM((4, 8, BLK, BLK), jnp.bfloat16),
            pltpu.VMEM((4, 8, BLK, BLK), jnp.bfloat16),
            pltpu.VMEM((8 * ROWS, NK * BLK), jnp.bfloat16),
            pltpu.VMEM((3, 4, 8 * ROWS, BLK), jnp.bfloat16),
            pltpu.VMEM((4, 8 * ROWS, BLK), jnp.bfloat16),
            pltpu.VMEM((4, 8 * ROWS, BLK), jnp.bfloat16),
            pltpu.VMEM((4, 8 * ROWS, BLK), jnp.bfloat16),
            pltpu.VMEM((4, 2, 8, 32, BLK), jnp.bfloat16),
            pltpu.VMEM((2, 4, 8, 32, BLK), jnp.bfloat16),
            dma((20,)), dma((3,)), dma((3,)), dma((3, 2)), dma((3, 2)), dma((3, NK)), dma((3, NK)),
            dma((4, 3, 2)), dma((4, 3, 2)), dma((3, 4)), dma((4,)), dma((2, 4)), dma((4, 2)), dma((2, 4)),
        ],
        compiler_params=pltpu.CompilerParams(collective_id=0, has_side_effects=True, vmem_limit_bytes=56 * 2**20),
        cost_estimate=pl.CostEstimate(flops=17_200_000_000, bytes_accessed=8_000_000, transcendentals=0),
    )(left_size, right_size, left_charge, right_charge, psi, left_ops, right_ops)
    return result[:, None]


def solution(mesh):
    in_specs = (P("sec", None, None, None), P("op", "sec", None, None), P("op", "sec", None, None), P(), P(), P(), P())
    return jax.shard_map(per_device, mesh=mesh, in_specs=in_specs, out_specs=P(None, "sec", "op", None), check_vma=False)
```

time: 306 us -> 108 us (0.35)
  waiting for transfers between devices: 150 us -> 0 us
  Pallas kernels: 0 us -> 105 us
  matrix products: 84.7 us -> 0 us
  other arithmetic: 21.2 us -> 0 us
  blocking collectives: 15.8 us -> 0 us
  local copies, waits for them, and re-layouts: 17.4 us -> 1.87 us
  between operations: 13.5 us -> 0.01 us
    pallas_call x0 -> x1, Pallas kernels: none -> 105 us  [per_device(): pl.pallas_call(kernel, out_shape=jax.ShapeDtypeStruct((32, 32, BLK), jnp....]
    all_gather x1 -> x0, waiting for transfers between devices: 97.2 us -> none  [per_device(): piece = lax.all_gather(right_ops, 'sec', axis=1, tiled=True)]
    dot_general x8 -> x0, matrix products: 84.7 us -> none  [one_term(): jnp.einsum('abil,bml->abim', inner, piece[index], preferred_element_type=...]
    reduce_scatter x1 -> x0, waiting for transfers between devices: 52.3 us -> none  [per_device(): lax.psum_scatter(total, 'op', scatter_dimension=2, tiled=True)]
    all_to_all x1 -> x0, blocking collectives: 15.8 us -> none  [per_device(): lax.all_to_all(banded, 'sec', split_axis=1, concat_axis=0, tiled=True)]
    mul x1 -> x0, other arithmetic: 10.6 us -> none  [per_device(): masked = psi * in_mask.astype(jnp.bfloat16)]
    while x1 -> x0, local copies, waits for them, and re-layouts: 10.5 us -> none  [per_device(): lax.fori_loop(0, op_count, one_term, jnp.zeros(masked.shape, jnp.float32))]
    select_n x1 -> x0, other arithmetic: 7.52 us -> none  [per_device(): total = jnp.where(in_mask, total, 0.0)]
  transfers between devices with their start and end apart: 2 -> 0, of which waited for: 2 -> 0; matrix products, arithmetic and copies ran while one was open for 6% -> 0% of each run, Pallas kernels for 0% -> 0%
where the time goes in v1:
time: 108 us; the launch traced here: 106 us
  Pallas kernels  105 us (97%)
  local copies, waits for them, and re-layouts  1.87 us (2%)
    pallas_call x1, Pallas kernels, per_device(): pl.pallas_call(kernel, out_shape=jax.ShapeDtypeStruct((32, 32, BLK), jnp....  105 us

profile of v1, /device:TPU:32, one launch (start us, length us, event | category | flops | bytes accessed | tf_op | source)
XLA Modules:
  0.0 106.5 jit_solution(15683120677801685545)
XLA Ops:
  0.0 104.6 %shard_map.73 = bf16[32,32,256]{2,1,0:T(8,128)(2,1)} custom-call(s32[32]{0:T(128)} %lsize.1, s32[16]{0:T(128)} %rsize.1, s32[32]{0:T(128)} %lcharge.1, s32[16]{0:T(128)} %rcharge.1, bf16[2,16,256,256]{3,2,1,0:T(8,128)(2,1)} %psi.1, bf16[8,2,256,256]{3,2,1,0:T(8,128)(2,1)} %left.1, bf16[8,1,256,256]{3,2,1,0:T(8,128)(2,1)} %right.1), custom_call_target="tpu_custom_call" | custom-call | flops 17200001024 | bytes 8000000 | tf_op jit(solution)/shard_map/pallas_call | solution.py:279
  104.6 1.9 %copy.10 = bf16[32,1,32,256]{3,2,1,0:T(8,128)(2,1)} copy(bf16[32,1,32,256]{3,2,1,0:T(8,128)(2,1)} %bitcast.3) | data formatting | bytes 1048576

commit v2 on v1

v2 whole, which is shorter than its diff:
```python
import jax
import jax.numpy as jnp
from jax import lax
from jax.experimental import pallas as pl
from jax.experimental.pallas import tpu as pltpu
from jax.sharding import PartitionSpec as P

MESH = pl.DeviceIdType.MESH
BLK = 256
NK = 8
ROWS = 64
HALF = 32
UNROLL = 4


def wrap(i):
    return lax.rem(i, 4)


def kernel(lsize, rsize, lcharge, rcharge, psi, left, right, out,
           lb, rb, pb, pm, inner, stage, far, near, mine, fin, got,
           own_sem, p_send, p_recv, px_send, px_recv, r_send, r_recv, l_send, l_recv,
           x_send, far_recv, x_recv, f_send, f_recv):
    op, sec = lax.axis_index("op"), lax.axis_index("sec")
    x, c = lax.div(op, 2), lax.rem(op, 2)
    z, y = lax.div(sec, 4), lax.rem(sec, 4)
    p, q = y + c * (z - y), z + c * (y - z)

    def sec_at(pp, qq):
        return 4 * qq + pp + 3 * c * (pp - qq)

    def dev(dx=0, dp=0, dq=0, other=False):
        core = 1 - c if other else c
        return (2 * wrap(x + dx) + core, sec_at(wrap(p + dp), wrap(q + dq)))

    def remote(src, dst, send, recv, to):
        return pltpu.make_async_remote_copy(src_ref=src, dst_ref=dst, send_sem=send, recv_sem=recv, device_id=to, device_id_type=MESH)

    barrier = pltpu.get_barrier_semaphore()
    senders = [dev(dp=s) for s in (1, 2, 3)] + [dev(dq=s) for s in (1, 2, 3)] + [dev(dx=s) for s in (1, 3)]
    senders += [dev(dp=s, other=True) for s in range(4)]
    for to in senders:
        pl.semaphore_signal(barrier, 1, device_id=to, device_id_type=MESH)

    def start_row(j, half):
        place = (wrap(x + 2) * ROWS + HALF * half, wrap(x + 1 + 2 * half) * ROWS + HALF * (1 - half), wrap(x + 1 + 2 * half) * ROWS + HALF * half, x * ROWS + HALF * half)[j]
        return pl.ds(pl.multiple_of(place, HALF), HALF)

    def half_rows(half):
        return pl.ds(HALF * half, HALF)

    own = [pltpu.make_async_copy(psi.at[:, sec_at(p, wrap(q + r))], pb.at[r, pl.ds(0, 2)], own_sem.at[r]) for r in range(4)]
    own += [pltpu.make_async_copy(right.at[k, 0], rb.at[0, :, pl.ds(k * BLK, BLK)], own_sem.at[4 + k]) for k in range(NK)]
    for j in range(4):
        for a in range(2):
            for h in range(2):
                own.append(pltpu.make_async_copy(left.at[:, a, start_row(j, h)], lb.at[j, a, :, half_rows(h)], own_sem.at[12 + 4 * j + 2 * a + h]))
    for copy in own:
        copy.start()

    pl.semaphore_wait(barrier, len(senders))

    sent = []

    def start(copy):
        copy.start()
        sent.append(copy)

    quarter = pl.ds(pl.multiple_of(x * ROWS, ROWS), ROWS)

    def p_copy(s, r):
        b = sec_at(wrap(p + s), wrap(q + r))
        if r == 0:
            return remote(psi.at[:, b], pb.at[0, pl.ds(2 * (4 - s), 2)], p_send.at[s - 1, 0], p_recv.at[3 - s, 0], dev(dp=s))
        return remote(psi.at[:, b, quarter], pb.at[r, pl.ds(2 * (4 - s), 2), quarter], p_send.at[s - 1, r], p_recv.at[3 - s, r], dev(dp=s))

    def r_copy(k, to_right):
        return remote(right.at[k, 0], rb.at[3 if to_right else 1, :, pl.ds(k * BLK, BLK)],
                      r_send.at[0 if to_right else 1, k], r_recv.at[2 if to_right else 0, k], dev(dq=1 if to_right else 3))

    def r_pass(k):
        here = rb.at[3 if k < 4 else 1, :, pl.ds(k * BLK, BLK)]
        return remote(here, rb.at[2, :, pl.ds(k * BLK, BLK)], r_send.at[2, k], r_recv.at[1, k], dev(dq=1 if k < 4 else 3))

    def l_copy(j, a, h, to_right):
        slot = 3 if to_right else 1
        return remote(left.at[:, a, start_row(j, h)], lb.at[j, 2 * slot + a, :, half_rows(h)],
                      l_send.at[j, 0 if to_right else 1, a, h], l_recv.at[j, slot - 1, a, h], dev(dp=1 if to_right else 3))

    def l_pass(j, a):
        here = lb.at[j, 2 * (3 if a == 0 else 1) + a]
        return remote(here, lb.at[j, 4 + a], l_send.at[j, 2, a, 0], l_recv.at[j, 1, a, 0], dev(dp=1 if a == 0 else 3))

    def l_start(j):
        for i in range(2):
            for h in range(2):
                start(l_copy(j, i, h, True))
                start(l_copy(j, 1 - i, h, False))

    def l_forward(j):
        for i in range(2):
            for h in range(2):
                l_copy(j, i, h, True).wait_recv()
            if i == 0:
                start(l_pass(j, 0))
            for h in range(2):
                l_copy(j, 1 - i, h, False).wait_recv()
            if i == 0:
                start(l_pass(j, 1))

    def px_view(slot_x, half):
        return pb.at[pl.ds(1, 3), pl.ds(2 + 3 * half, 3), pl.ds(pl.multiple_of(wrap(x + slot_x) * ROWS, ROWS), ROWS)]

    def px_copy(half, to_right):
        return remote(px_view(0, half), px_view(0, half), px_send.at[0 if to_right else 1, half], px_recv.at[2 if to_right else 0, half],
                      dev(dx=1 if to_right else 3))

    def px_pass(half):
        slot_x = 3 if half == 0 else 1
        return remote(px_view(slot_x, half), px_view(slot_x, half), px_send.at[2, half], px_recv.at[1, half], dev(dx=1 if half == 0 else 3))

    def px_arrive(slot_x, half):
        return remote(px_view(slot_x, half), px_view(slot_x, half), px_send.at[2, half], px_recv.at[slot_x - 1, half], dev(dx=1))

    row_at = lax.broadcasted_iota(jnp.int32, (BLK, BLK), 0)
    col_at = lax.broadcasted_iota(jnp.int32, (BLK, BLK), 1)

    def mask_block(n, _):
        r, sa = lax.div(n, 8), lax.rem(n, 8)
        a = 2 * sec_at(wrap(p + lax.div(sa, 2)), q) + lax.rem(sa, 2)
        b = sec_at(p, wrap(q + r))
        live = (row_at < lsize[a]) & (col_at < rsize[b])
        block = pb[r, sa].astype(jnp.float32)
        pm[r, sa] = jnp.where(live, block, 0.0).astype(jnp.bfloat16)
        return 0

    def product(j, r):
        def first(sa, _):
            lhs = lb[j, sa].reshape(NK * ROWS, BLK)
            part = jnp.dot(lhs, pm[r, sa], preferred_element_type=jnp.float32).astype(jnp.bfloat16)
            here = pl.ds(pl.multiple_of(sa * ROWS, ROWS), ROWS)
            for k in range(NK):
                inner[here, k * BLK:(k + 1) * BLK] = part[k * ROWS:(k + 1) * ROWS]
            return 0

        lax.fori_loop(0, 8, first, 0, unroll=UNROLL)
        total = lax.dot_general(inner[...], rb[r], (((1,), (1,)), ((), ())), preferred_element_type=jnp.float32)
        return total.reshape(8, ROWS, BLK)

    def far_copy(side, r):
        return remote(stage.at[0, side, r], far.at[side, r], x_send.at[0, side, r], far_recv.at[side, r], dev(dx=(1, 3)[side]))

    def x_copy(j, side, r):
        return remote(stage.at[j, side, r], near.at[j - 1, side, r], x_send.at[j, side, r], x_recv.at[j - 1, side, r], dev(dx=(1, 3)[side]))

    def fin_copy(r, other):
        core = 1 - c if other else c
        return remote(fin.at[r, core], got.at[c, wrap(4 - r)], f_send.at[r, 1 if other else 0], f_recv.at[c, wrap(4 - r)], dev(dq=r, other=other))

    def halves(total):
        return total[:, :HALF], total[:, HALF:]

    def stage_far(r):
        for side, part in enumerate(halves(product(0, r))):
            stage[0, side, r] = part.astype(jnp.bfloat16)
            far_copy(side, r).start()

    def stage_one(r):
        for side, part in enumerate(halves(product(1, r))):
            stage[1, side, r] = part.astype(jnp.bfloat16)
            x_copy(1, side, r).start()

    def stage_two(r):
        parts = halves(product(2, r))
        for side in range(2):
            far_copy(side, r).wait_recv()
            stage[2, side, r] = (parts[side] + far[side, r].astype(jnp.float32)).astype(jnp.bfloat16)
            x_copy(2, side, r).start()

    def stage_own(r):
        mine[r] = product(3, r)

    def slot_order(n):
        return n + lax.div(n, 2) * (5 - 2 * n)

    def run(body, low):
        def step(n, _):
            body(slot_order(n))
            return 0

        lax.fori_loop(low, 4, step, 0)

    for s in (1, 3, 2):
        for r in (1, 2, 3):
            start(p_copy(s, r))
    for s in (1, 3, 2):
        start(p_copy(s, 0))
    l_start(0)
    for i in range(NK):
        start(r_copy(i, True))
        start(r_copy(NK - 1 - i, False))
    for s in (1, 3, 2):
        for r in (1, 2, 3):
            p_copy(s, r).wait_recv()
    for i in range(2):
        start(px_copy(i, True))
        start(px_copy(1 - i, False))
    for copy in own:
        copy.wait()
    for s in (1, 3, 2):
        p_copy(s, 0).wait_recv()
    lax.fori_loop(0, 8, mask_block, 0)
    l_forward(0)
    px_arrive(3, 0).wait_recv()
    start(px_pass(0))
    px_arrive(1, 1).wait_recv()
    start(px_pass(1))
    for i in range(4):
        r_copy(i, True).wait_recv()
        start(r_pass(i))
        r_copy(NK - 1 - i, False).wait_recv()
        start(r_pass(NK - 1 - i))
    l_start(1)
    l_pass(0, 0).wait_recv()
    l_pass(0, 1).wait_recv()
    stage_far(0)
    px_arrive(3, 1).wait_recv()
    px_arrive(1, 0).wait_recv()
    px_arrive(2, 0).wait_recv()
    px_arrive(2, 1).wait_recv()
    lax.fori_loop(8, 32, mask_block, 0)
    for i in range(4, NK):
        r_copy(i, True).wait_recv()
        r_copy(NK - 1 - i, False).wait_recv()
    l_start(2)
    for k in range(NK):
        r_pass(k).wait_recv()
    run(stage_far, 1)
    l_forward(1)
    l_start(3)
    for j, body in ((1, stage_one), (2, stage_two), (3, stage_own)):
        if j < 3:
            l_forward(j + 1)
        l_pass(j, 0).wait_recv()
        l_pass(j, 1).wait_recv()
        run(body, 0)

    def close(r):
        for h in range(2):
            x_copy(2 - h, 0, r).wait_recv()
            x_copy(1 + h, 1, r).wait_recv()
            total = mine[r, :, HALF * h:HALF * (h + 1)] + near[1 - h, 0, r].astype(jnp.float32) + near[h, 1, r].astype(jnp.float32)
            fin[r, h] = total.astype(jnp.bfloat16)
        fin_copy(r, True).start()

        @pl.when(r > 0)
        def _():
            fin_copy(r, False).start()

    run(close, 0)

    got[c, 0] = fin[0, c]

    def arrived(part, slot):
        return remote(fin.at[0, 0], got.at[part, slot], f_send.at[0, 0], f_recv.at[part, slot], dev(dq=1))

    for s in range(4):
        arrived(1 - c, s).wait_recv()
    for s in range(1, 4):
        arrived(c, s).wait_recv()

    row_at = lax.broadcasted_iota(jnp.int32, (32, BLK), 0) + 32 * op
    col_live = lax.broadcasted_iota(jnp.int32, (32, BLK), 1) < rsize[sec]

    def finish(n, _):
        sz, sy, i = lax.div(n, 8), lax.rem(lax.div(n, 2), 4), lax.rem(n, 2)
        a = 2 * (4 * wrap(z + sz) + wrap(y + sy)) + i
        total = got[0, sz, 2 * sy + i].astype(jnp.float32) + got[1, sy, 2 * sz + i].astype(jnp.float32)
        rows = jnp.where(jnp.abs(lcharge[a] - rcharge[sec]) <= 1, lsize[a], 0)
        out[a] = jnp.where((row_at < rows) & col_live, total, 0.0).astype(jnp.bfloat16)
        return 0

    lax.fori_loop(0, 32, finish, 0)

    for copy in sent:
        copy.wait_send()

    def drain(r, _):
        for side in range(2):
            far_copy(side, r).wait_send()
            x_copy(1, side, r).wait_send()
            x_copy(2, side, r).wait_send()
        fin_copy(r, True).wait_send()
        return 0

    lax.fori_loop(0, 4, drain, 0)
    for r in range(1, 4):
        fin_copy(r, False).wait_send()


def per_device(psi, left_ops, right_ops, left_size, right_size, left_charge, right_charge):
    smem = pl.BlockSpec(memory_space=pltpu.SMEM)
    hbm = pl.BlockSpec(memory_space=pl.ANY)
    dma = pltpu.SemaphoreType.DMA
    result = pl.pallas_call(
        kernel,
        out_shape=jax.ShapeDtypeStruct((32, 32, BLK), jnp.bfloat16),
        in_specs=[smem] * 4 + [hbm] * 3,
        out_specs=pl.BlockSpec(memory_space=pltpu.VMEM),
        scratch_shapes=[
            pltpu.VMEM((4, 8, NK, ROWS, BLK), jnp.bfloat16),
            pltpu.VMEM((4, BLK, NK * BLK), jnp.bfloat16),
            pltpu.VMEM((4, 8, BLK, BLK), jnp.bfloat16),
            pltpu.VMEM((4, 8, BLK, BLK), jnp.bfloat16),
            pltpu.VMEM((8 * ROWS, NK * BLK), jnp.bfloat16),
            pltpu.VMEM((3, 2, 4, 8, HALF, BLK), jnp.bfloat16),
            pltpu.VMEM((2, 4, 8, HALF, BLK), jnp.bfloat16),
            pltpu.VMEM((2, 2, 4, 8, HALF, BLK), jnp.bfloat16),
            pltpu.VMEM((4, 8, ROWS, BLK), jnp.float32),
            pltpu.VMEM((4, 2, 8, HALF, BLK), jnp.bfloat16),
            pltpu.VMEM((2, 4, 8, HALF, BLK), jnp.bfloat16),
            dma((28,)), dma((3, 4)), dma((3, 4)), dma((3, 2)), dma((3, 2)), dma((3, NK)), dma((3, NK)),
            dma((4, 3, 2, 2)), dma((4, 3, 2, 2)), dma((3, 2, 4)), dma((2, 4)), dma((2, 2, 4)), dma((4, 2)), dma((2, 4)),
        ],
        compiler_params=pltpu.CompilerParams(collective_id=0, has_side_effects=True, vmem_limit_bytes=56 * 2**20),
        cost_estimate=pl.CostEstimate(flops=17_200_000_000, bytes_accessed=8_000_000, transcendentals=0),
    )(left_size, right_size, left_charge, right_charge, psi, left_ops, right_ops)
    return result[:, None]


def solution(mesh):
    in_specs = (P("sec", None, None, None), P("op", "sec", None, None), P("op", "sec", None, None), P(), P(), P(), P())
    return jax.shard_map(per_device, mesh=mesh, in_specs=in_specs, out_specs=P(None, "sec", "op", None), check_vma=False)
```

time: 108 us -> 99.4 us (0.920); the launches traced: 106 us -> 99.3 us
  Pallas kernels: 105 us -> 97.4 us
    pallas_call x1, Pallas kernels: 105 us -> 97.4 us  [per_device(): pl.pallas_call(kernel, out_shape=jax.ShapeDtypeStruct((32, 32, BLK), jnp....]
where the time goes in v2:
time: 99.4 us; the launch traced here: 99.3 us
  Pallas kernels  97.4 us (98%)
  local copies, waits for them, and re-layouts  1.87 us (2%)
    pallas_call x1, Pallas kernels, per_device(): pl.pallas_call(kernel, out_shape=jax.ShapeDtypeStruct((32, 32, BLK), jnp....  97.4 us

profile of v2, /device:TPU:32, one launch (start us, length us, event | category | flops | bytes accessed | tf_op | source)
XLA Modules:
  0.0 99.3 jit_solution(1549575183234966735)
XLA Ops:
  0.0 97.4 %shard_map.73 = bf16[32,32,256]{2,1,0:T(8,128)(2,1)} custom-call(s32[32]{0:T(128)} %lsize.1, s32[16]{0:T(128)} %rsize.1, s32[32]{0:T(128)} %lcharge.1, s32[16]{0:T(128)} %rcharge.1, bf16[2,16,256,256]{3,2,1,0:T(8,128)(2,1)} %psi.1, bf16[8,2,256,256]{3,2,1,0:T(8,128)(2,1)} %left.1, bf16[8,1,256,256]{3,2,1,0:T(8,128)(2,1)} %right.1), custom_call_target="tpu_custom_call" | custom-call | flops 17200001024 | bytes 8000000 | tf_op jit(solution)/shard_map/pallas_call | solution.py:305
  97.4 1.9 %copy.10 = bf16[32,1,32,256]{3,2,1,0:T(8,128)(2,1)} copy(bf16[32,1,32,256]{3,2,1,0:T(8,128)(2,1)} %bitcast.3) | data formatting | bytes 1048576

commit v3 on v2

--- a/solution.py
+++ b/solution.py
@@ -10,7 +10,6 @@
 NK = 8
 ROWS = 64
 HALF = 32
-UNROLL = 4
 
 
 def wrap(i):
@@ -66,13 +65,8 @@
         copy.start()
         sent.append(copy)
 
-    quarter = pl.ds(pl.multiple_of(x * ROWS, ROWS), ROWS)
-
-    def p_copy(s, r):
-        b = sec_at(wrap(p + s), wrap(q + r))
-        if r == 0:
-            return remote(psi.at[:, b], pb.at[0, pl.ds(2 * (4 - s), 2)], p_send.at[s - 1, 0], p_recv.at[3 - s, 0], dev(dp=s))
-        return remote(psi.at[:, b, quarter], pb.at[r, pl.ds(2 * (4 - s), 2), quarter], p_send.at[s - 1, r], p_recv.at[3 - s, r], dev(dp=s))
+    def p_copy(s):
+        return remote(psi.at[:, sec_at(wrap(p + s), wrap(q + x))], pb.at[x, pl.ds(2 * (4 - s), 2)], p_send.at[s - 1], p_recv.at[3 - s], dev(dp=s))
 
     def r_copy(k, to_right):
         return remote(right.at[k, 0], rb.at[3 if to_right else 1, :, pl.ds(k * BLK, BLK)],
@@ -108,25 +102,27 @@
             if i == 0:
                 start(l_pass(j, 1))
 
-    def px_view(slot_x, half):
-        return pb.at[pl.ds(1, 3), pl.ds(2 + 3 * half, 3), pl.ds(pl.multiple_of(wrap(x + slot_x) * ROWS, ROWS), ROWS)]
-
-    def px_copy(half, to_right):
-        return remote(px_view(0, half), px_view(0, half), px_send.at[0 if to_right else 1, half], px_recv.at[2 if to_right else 0, half],
+    def px_view(slot_x, piece):
+        return pb.at[wrap(x + slot_x), pl.ds((2, 6, 4, 5)[piece], 2 if piece < 2 else 1)]
+
+    def px_copy(piece, to_right):
+        return remote(px_view(0, piece), px_view(0, piece), px_send.at[0 if to_right else 1, piece], px_recv.at[2 if to_right else 0, piece],
                       dev(dx=1 if to_right else 3))
 
-    def px_pass(half):
-        slot_x = 3 if half == 0 else 1
-        return remote(px_view(slot_x, half), px_view(slot_x, half), px_send.at[2, half], px_recv.at[1, half], dev(dx=1 if half == 0 else 3))
-
-    def px_arrive(slot_x, half):
-        return remote(px_view(slot_x, half), px_view(slot_x, half), px_send.at[2, half], px_recv.at[slot_x - 1, half], dev(dx=1))
+    def px_pass(piece):
+        slot_x = 3 if piece % 2 == 0 else 1
+        return remote(px_view(slot_x, piece), px_view(slot_x, piece), px_send.at[2, piece], px_recv.at[1, piece], dev(dx=1 if piece % 2 == 0 else 3))
+
+    def px_arrive(slot_x, piece):
+        return remote(px_view(slot_x, piece), px_view(slot_x, piece), px_send.at[2, piece], px_recv.at[slot_x - 1, piece], dev(dx=1))
 
     row_at = lax.broadcasted_iota(jnp.int32, (BLK, BLK), 0)
     col_at = lax.broadcasted_iota(jnp.int32, (BLK, BLK), 1)
 
-    def mask_block(n, _):
-        r, sa = lax.div(n, 8), lax.rem(n, 8)
+    def mask_slot(d):
+        lax.fori_loop(0, 8, lambda sa, _: mask_block(wrap(x + d), sa), 0)
+
+    def mask_block(r, sa):
         a = 2 * sec_at(wrap(p + lax.div(sa, 2)), q) + lax.rem(sa, 2)
         b = sec_at(p, wrap(q + r))
         live = (row_at < lsize[a]) & (col_at < rsize[b])
@@ -134,17 +130,23 @@
         pm[r, sa] = jnp.where(live, block, 0.0).astype(jnp.bfloat16)
         return 0
 
-    def product(j, r):
-        def first(sa, _):
-            lhs = lb[j, sa].reshape(NK * ROWS, BLK)
-            part = jnp.dot(lhs, pm[r, sa], preferred_element_type=jnp.float32).astype(jnp.bfloat16)
-            here = pl.ds(pl.multiple_of(sa * ROWS, ROWS), ROWS)
-            for k in range(NK):
-                inner[here, k * BLK:(k + 1) * BLK] = part[k * ROWS:(k + 1) * ROWS]
+    def slot_order(n):
+        return n + lax.div(n, 2) * (5 - 2 * n)
+
+    def first(j, sectors, begin=0, end=4):
+        def step(n, _):
+            r = wrap(x + slot_order(n))
+            for sa in sectors:
+                lhs = lb[j, sa].reshape(NK * ROWS, BLK)
+                part = jnp.dot(lhs, pm[r, sa], preferred_element_type=jnp.float32).astype(jnp.bfloat16)
+                for k in range(NK):
+                    inner[r, sa * ROWS:(sa + 1) * ROWS, k * BLK:(k + 1) * BLK] = part[k * ROWS:(k + 1) * ROWS]
             return 0
 
-        lax.fori_loop(0, 8, first, 0, unroll=UNROLL)
-        total = lax.dot_general(inner[...], rb[r], (((1,), (1,)), ((), ())), preferred_element_type=jnp.float32)
+        lax.fori_loop(begin, end, step, 0)
+
+    def product(r):
+        total = lax.dot_general(inner[r], rb[r], (((1,), (1,)), ((), ())), preferred_element_type=jnp.float32)
         return total.reshape(8, ROWS, BLK)
 
     def far_copy(side, r):
@@ -161,89 +163,102 @@
         return total[:, :HALF], total[:, HALF:]
 
     def stage_far(r):
-        for side, part in enumerate(halves(product(0, r))):
+        for side, part in enumerate(halves(product(r))):
             stage[0, side, r] = part.astype(jnp.bfloat16)
             far_copy(side, r).start()
 
     def stage_one(r):
-        for side, part in enumerate(halves(product(1, r))):
+        for side, part in enumerate(halves(product(r))):
             stage[1, side, r] = part.astype(jnp.bfloat16)
             x_copy(1, side, r).start()
 
     def stage_two(r):
-        parts = halves(product(2, r))
+        parts = halves(product(r))
         for side in range(2):
             far_copy(side, r).wait_recv()
             stage[2, side, r] = (parts[side] + far[side, r].astype(jnp.float32)).astype(jnp.bfloat16)
             x_copy(2, side, r).start()
 
     def stage_own(r):
-        mine[r] = product(3, r)
-
-    def slot_order(n):
-        return n + lax.div(n, 2) * (5 - 2 * n)
-
-    def run(body, low):
+        mine[r] = product(r)
+
+    def run(body, low, high, down=False):
         def step(n, _):
-            body(slot_order(n))
+            body(3 - n if down else wrap(x + slot_order(n)))
             return 0
 
-        lax.fori_loop(low, 4, step, 0)
+        lax.fori_loop(low, high, step, 0)
 
     for s in (1, 3, 2):
-        for r in (1, 2, 3):
-            start(p_copy(s, r))
-    for s in (1, 3, 2):
-        start(p_copy(s, 0))
-    l_start(0)
+        start(p_copy(s))
+    for s in (1, 3):
+        p_copy(s).wait_recv()
+    for piece in range(2):
+        start(px_copy(piece, True))
+        start(px_copy(1 - piece, False))
     for i in range(NK):
         start(r_copy(i, True))
         start(r_copy(NK - 1 - i, False))
-    for s in (1, 3, 2):
-        for r in (1, 2, 3):
-            p_copy(s, r).wait_recv()
-    for i in range(2):
-        start(px_copy(i, True))
-        start(px_copy(1 - i, False))
+    p_copy(2).wait_recv()
+    for piece in range(2, 4):
+        start(px_copy(piece, True))
+        start(px_copy(5 - piece, False))
     for copy in own:
         copy.wait()
-    for s in (1, 3, 2):
-        p_copy(s, 0).wait_recv()
-    lax.fori_loop(0, 8, mask_block, 0)
-    l_forward(0)
-    px_arrive(3, 0).wait_recv()
-    start(px_pass(0))
-    px_arrive(1, 1).wait_recv()
-    start(px_pass(1))
+    mask_slot(0)
     for i in range(4):
         r_copy(i, True).wait_recv()
         start(r_pass(i))
         r_copy(NK - 1 - i, False).wait_recv()
         start(r_pass(NK - 1 - i))
-    l_start(1)
-    l_pass(0, 0).wait_recv()
-    l_pass(0, 1).wait_recv()
-    stage_far(0)
-    px_arrive(3, 1).wait_recv()
-    px_arrive(1, 0).wait_recv()
-    px_arrive(2, 0).wait_recv()
-    px_arrive(2, 1).wait_recv()
-    lax.fori_loop(8, 32, mask_block, 0)
+    l_start(0)
+    for piece in (0, 1):
+        px_arrive(3 - 2 * (piece % 2), piece).wait_recv()
+        start(px_pass(piece))
+    for piece in (2, 3):
+        px_arrive(3 - 2 * (piece % 2), piece).wait_recv()
+        start(px_pass(piece))
     for i in range(4, NK):
         r_copy(i, True).wait_recv()
         r_copy(NK - 1 - i, False).wait_recv()
-    l_start(2)
+    l_forward(0)
+    l_start(1)
+    for piece in range(4):
+        px_arrive(1 + 2 * (piece % 2), piece).wait_recv()
+    mask_slot(1)
+    mask_slot(3)
+    first(0, (0, 1, 2, 3, 6, 7), 0, 3)
+    l_pass(0, 0).wait_recv()
+    l_pass(0, 1).wait_recv()
+    first(0, (4, 5), 0, 3)
     for k in range(NK):
         r_pass(k).wait_recv()
-    run(stage_far, 1)
     l_forward(1)
+    l_start(2)
+    run(stage_far, 0, 3)
+    for piece in range(4):
+        px_arrive(2, piece).wait_recv()
+    mask_slot(2)
+    first(0, range(8), 3, 4)
+    run(stage_far, 3, 4)
+    first(1, (0, 1, 2, 3, 6, 7))
+    l_pass(1, 0).wait_recv()
+    l_pass(1, 1).wait_recv()
+    first(1, (4, 5))
+    l_forward(2)
     l_start(3)
-    for j, body in ((1, stage_one), (2, stage_two), (3, stage_own)):
-        if j < 3:
-            l_forward(j + 1)
-        l_pass(j, 0).wait_recv()
-        l_pass(j, 1).wait_recv()
-        run(body, 0)
+    run(stage_one, 0, 4)
+    first(2, (0, 1, 2, 3, 6, 7))
+    l_pass(2, 0).wait_recv()
+    l_pass(2, 1).wait_recv()
+    first(2, (4, 5))
+    l_forward(3)
+    run(stage_two, 0, 4, True)
+    first(3, (0, 1, 2, 3, 6, 7))
+    l_pass(3, 0).wait_recv()
+    l_pass(3, 1).wait_recv()
+    first(3, (4, 5))
+    run(stage_own, 0, 4)
 
     def close(r):
         for h in range(2):
@@ -257,7 +272,7 @@
         def _():
             fin_copy(r, False).start()
 
-    run(close, 0)
+    run(close, 0, 4, True)
 
     got[c, 0] = fin[0, c]
 
@@ -312,14 +327,14 @@
             pltpu.VMEM((4, BLK, NK * BLK), jnp.bfloat16),
             pltpu.VMEM((4, 8, BLK, BLK), jnp.bfloat16),
             pltpu.VMEM((4, 8, BLK, BLK), jnp.bfloat16),
-            pltpu.VMEM((8 * ROWS, NK * BLK), jnp.bfloat16),
+            pltpu.VMEM((4, 8 * ROWS, NK * BLK), jnp.bfloat16),
             pltpu.VMEM((3, 2, 4, 8, HALF, BLK), jnp.bfloat16),
             pltpu.VMEM((2, 4, 8, HALF, BLK), jnp.bfloat16),
             pltpu.VMEM((2, 2, 4, 8, HALF, BLK), jnp.bfloat16),
             pltpu.VMEM((4, 8, ROWS, BLK), jnp.float32),
             pltpu.VMEM((4, 2, 8, HALF, BLK), jnp.bfloat16),
             pltpu.VMEM((2, 4, 8, HALF, BLK), jnp.bfloat16),
-            dma((28,)), dma((3, 4)), dma((3, 4)), dma((3, 2)), dma((3, 2)), dma((3, NK)), dma((3, NK)),
+            dma((28,)), dma((3,)), dma((3,)), dma((3, 4)), dma((3, 4)), dma((3, NK)), dma((3, NK)),
             dma((4, 3, 2, 2)), dma((4, 3, 2, 2)), dma((3, 2, 4)), dma((2, 4)), dma((2, 2, 4)), dma((4, 2)), dma((2, 4)),
         ],
         compiler_params=pltpu.CompilerParams(collective_id=0, has_side_effects=True, vmem_limit_bytes=56 * 2**20),

time: 99.4 us -> 94.7 us (0.953)
  Pallas kernels: 97.4 us -> 92.6 us
    pallas_call x1, Pallas kernels: 97.4 us -> 92.6 us  [per_device(): pl.pallas_call(kernel, out_shape=jax.ShapeDtypeStruct((32, 32, BLK), jnp....]
where the time goes in v3:
time: 94.7 us; the launch traced here: 94.5 us
  Pallas kernels  92.6 us (98%)
  local copies, waits for them, and re-layouts  1.87 us (2%)
    pallas_call x1, Pallas kernels, per_device(): pl.pallas_call(kernel, out_shape=jax.ShapeDtypeStruct((32, 32, BLK), jnp....  92.6 us

profile of v3, /device:TPU:32, one launch (start us, length us, event | category | flops | bytes accessed | tf_op | source)
XLA Modules:
  0.0 94.5 jit_solution(14711420180752648460)
XLA Ops:
  0.0 92.6 %shard_map.73 = bf16[32,32,256]{2,1,0:T(8,128)(2,1)} custom-call(s32[32]{0:T(128)} %lsize.1, s32[16]{0:T(128)} %rsize.1, s32[32]{0:T(128)} %lcharge.1, s32[16]{0:T(128)} %rcharge.1, bf16[2,16,256,256]{3,2,1,0:T(8,128)(2,1)} %psi.1, bf16[8,2,256,256]{3,2,1,0:T(8,128)(2,1)} %left.1, bf16[8,1,256,256]{3,2,1,0:T(8,128)(2,1)} %right.1), custom_call_target="tpu_custom_call" | custom-call | flops 17200001024 | bytes 8000000 | tf_op jit(solution)/shard_map/pallas_call | solution.py:320
  92.7 1.9 %copy.10 = bf16[32,1,32,256]{3,2,1,0:T(8,128)(2,1)} copy(bf16[32,1,32,256]{3,2,1,0:T(8,128)(2,1)} %bitcast.3) | data formatting | bytes 1048576

commit v4 on v3

--- a/solution.py
+++ b/solution.py
@@ -17,7 +17,7 @@
 
 
 def kernel(lsize, rsize, lcharge, rcharge, psi, left, right, out,
-           lb, rb, pb, pm, inner, stage, far, near, mine, fin, got,
+           lb, rb, pb, pm, inner, stage, far, near, fin, got,
            own_sem, p_send, p_recv, px_send, px_recv, r_send, r_recv, l_send, l_recv,
            x_send, far_recv, x_recv, f_send, f_recv):
     op, sec = lax.axis_index("op"), lax.axis_index("sec")
@@ -81,9 +81,10 @@
         return remote(left.at[:, a, start_row(j, h)], lb.at[j, 2 * slot + a, :, half_rows(h)],
                       l_send.at[j, 0 if to_right else 1, a, h], l_recv.at[j, slot - 1, a, h], dev(dp=1 if to_right else 3))
 
-    def l_pass(j, a):
-        here = lb.at[j, 2 * (3 if a == 0 else 1) + a]
-        return remote(here, lb.at[j, 4 + a], l_send.at[j, 2, a, 0], l_recv.at[j, 1, a, 0], dev(dp=1 if a == 0 else 3))
+    def l_pass(j, a, piece):
+        pair = pl.ds(2 * piece, 2)
+        here = lb.at[j, 2 * (3 if a == 0 else 1) + a, pair]
+        return remote(here, lb.at[j, 4 + a, pair], l_send.at[j, 2, a, piece], l_recv.at[j, 1, a, piece], dev(dp=1 if a == 0 else 3))
 
     def l_start(j):
         for i in range(2):
@@ -96,11 +97,13 @@
             for h in range(2):
                 l_copy(j, i, h, True).wait_recv()
             if i == 0:
-                start(l_pass(j, 0))
+                for piece in range(4):
+                    start(l_pass(j, 0, piece))
             for h in range(2):
                 l_copy(j, 1 - i, h, False).wait_recv()
             if i == 0:
-                start(l_pass(j, 1))
+                for piece in range(4):
+                    start(l_pass(j, 1, piece))
 
     def px_view(slot_x, piece):
         return pb.at[wrap(x + slot_x), pl.ds((2, 6, 4, 5)[piece], 2 if piece < 2 else 1)]
@@ -120,7 +123,10 @@
     col_at = lax.broadcasted_iota(jnp.int32, (BLK, BLK), 1)
 
     def mask_slot(d):
-        lax.fori_loop(0, 8, lambda sa, _: mask_block(wrap(x + d), sa), 0)
+        lax.fori_loop(2, 8, lambda sa, _: mask_block(wrap(x + d), sa), 0)
+
+    def mask_own():
+        lax.fori_loop(0, 8, lambda n, _: mask_block(lax.div(n, 2), lax.rem(n, 2)), 0)
 
     def mask_block(r, sa):
         a = 2 * sec_at(wrap(p + lax.div(sa, 2)), q) + lax.rem(sa, 2)
@@ -132,6 +138,10 @@
 
     def slot_order(n):
         return n + lax.div(n, 2) * (5 - 2 * n)
+
+    def far_order(n):
+        power = 1 + 3 * x + lax.div(9 * x * (x - 1), 2) + lax.div(27 * x * (x - 1) * (x - 2), 6)
+        return lax.rem(lax.div((212, 49, 171, 78)[n], power), 4)
 
     def first(j, sectors, begin=0, end=4):
         def step(n, _):
@@ -143,7 +153,8 @@
                     inner[r, sa * ROWS:(sa + 1) * ROWS, k * BLK:(k + 1) * BLK] = part[k * ROWS:(k + 1) * ROWS]
             return 0
 
-        lax.fori_loop(begin, end, step, 0)
+        steps = end - begin
+        lax.fori_loop(begin, end, step, 0, unroll=steps if steps < 4 or len(sectors) < 4 else 2)
 
     def product(r):
         total = lax.dot_general(inner[r], rb[r], (((1,), (1,)), ((), ())), preferred_element_type=jnp.float32)
@@ -180,17 +191,31 @@
             x_copy(2, side, r).start()
 
     def stage_own(r):
-        mine[r] = product(r)
+        parts = halves(product(r))
+        for h in range(2):
+            x_copy(2 - h, 0, r).wait_recv()
+            x_copy(1 + h, 1, r).wait_recv()
+            total = parts[h] + near[1 - h, 0, r].astype(jnp.float32) + near[h, 1, r].astype(jnp.float32)
+            fin[r, h] = total.astype(jnp.bfloat16)
+        fin_copy(r, True).start()
+
+        @pl.when(r > 0)
+        def _():
+            fin_copy(r, False).start()
 
     def run(body, low, high, down=False):
         def step(n, _):
             body(3 - n if down else wrap(x + slot_order(n)))
             return 0
 
-        lax.fori_loop(low, high, step, 0)
+        lax.fori_loop(low, high, step, 0, unroll=2 if (high - low) % 2 == 0 else 1)
 
     for s in (1, 3, 2):
         start(p_copy(s))
+    for copy in own:
+        copy.wait()
+    mask_own()
+    first(0, (0, 1))
     for s in (1, 3):
         p_copy(s).wait_recv()
     for piece in range(2):
@@ -203,8 +228,6 @@
     for piece in range(2, 4):
         start(px_copy(piece, True))
         start(px_copy(5 - piece, False))
-    for copy in own:
-        copy.wait()
     mask_slot(0)
     for i in range(4):
         r_copy(i, True).wait_recv()
@@ -227,54 +250,58 @@
         px_arrive(1 + 2 * (piece % 2), piece).wait_recv()
     mask_slot(1)
     mask_slot(3)
-    first(0, (0, 1, 2, 3, 6, 7), 0, 3)
-    l_pass(0, 0).wait_recv()
-    l_pass(0, 1).wait_recv()
+    first(0, (2, 3, 6, 7), 0, 3)
+    for piece in range(4):
+        l_pass(0, 0, piece).wait_recv()
+        l_pass(0, 1, piece).wait_recv()
     first(0, (4, 5), 0, 3)
+    for n in (0, 1):
+        stage_far(far_order(n))
     for k in range(NK):
         r_pass(k).wait_recv()
     l_forward(1)
     l_start(2)
-    run(stage_far, 0, 3)
     for piece in range(4):
         px_arrive(2, piece).wait_recv()
     mask_slot(2)
-    first(0, range(8), 3, 4)
-    run(stage_far, 3, 4)
+    first(0, range(2, 8), 3, 4)
+    for n in (2, 3):
+        stage_far(far_order(n))
     first(1, (0, 1, 2, 3, 6, 7))
-    l_pass(1, 0).wait_recv()
-    l_pass(1, 1).wait_recv()
+    for piece in range(4):
+        l_pass(1, 0, piece).wait_recv()
+        l_pass(1, 1, piece).wait_recv()
     first(1, (4, 5))
     l_forward(2)
     l_start(3)
     run(stage_one, 0, 4)
     first(2, (0, 1, 2, 3, 6, 7))
-    l_pass(2, 0).wait_recv()
-    l_pass(2, 1).wait_recv()
+    for piece in range(4):
+        l_pass(2, 0, piece).wait_recv()
+        l_pass(2, 1, piece).wait_recv()
     first(2, (4, 5))
     l_forward(3)
     run(stage_two, 0, 4, True)
     first(3, (0, 1, 2, 3, 6, 7))
-    l_pass(3, 0).wait_recv()
-    l_pass(3, 1).wait_recv()
+    for piece in range(4):
+        l_pass(3, 0, piece).wait_recv()
+        l_pass(3, 1, piece).wait_recv()
     first(3, (4, 5))
-    run(stage_own, 0, 4)
-
-    def close(r):
-        for h in range(2):
-            x_copy(2 - h, 0, r).wait_recv()
-            x_copy(1 + h, 1, r).wait_recv()
-            total = mine[r, :, HALF * h:HALF * (h + 1)] + near[1 - h, 0, r].astype(jnp.float32) + near[h, 1, r].astype(jnp.float32)
-            fin[r, h] = total.astype(jnp.bfloat16)
-        fin_copy(r, True).start()
-
-        @pl.when(r > 0)
-        def _():
-            fin_copy(r, False).start()
-
-    run(close, 0, 4, True)
+    run(stage_own, 0, 4, True)
 
     got[c, 0] = fin[0, c]
+
+    for copy in sent:
+        copy.wait_send()
+
+    def drain(r, _):
+        for side in range(2):
+            far_copy(side, r).wait_send()
+            x_copy(1, side, r).wait_send()
+            x_copy(2, side, r).wait_send()
+        return 0
+
+    lax.fori_loop(0, 4, drain, 0)
 
     def arrived(part, slot):
         return remote(fin.at[0, 0], got.at[part, slot], f_send.at[0, 0], f_recv.at[part, slot], dev(dq=1))
@@ -295,20 +322,10 @@
         out[a] = jnp.where((row_at < rows) & col_live, total, 0.0).astype(jnp.bfloat16)
         return 0
 
-    lax.fori_loop(0, 32, finish, 0)
-
-    for copy in sent:
-        copy.wait_send()
-
-    def drain(r, _):
-        for side in range(2):
-            far_copy(side, r).wait_send()
-            x_copy(1, side, r).wait_send()
-            x_copy(2, side, r).wait_send()
+    lax.fori_loop(0, 32, finish, 0, unroll=4)
+
+    for r in range(4):
         fin_copy(r, True).wait_send()
-        return 0
-
-    lax.fori_loop(0, 4, drain, 0)
     for r in range(1, 4):
         fin_copy(r, False).wait_send()
 
@@ -331,11 +348,10 @@
             pltpu.VMEM((3, 2, 4, 8, HALF, BLK), jnp.bfloat16),
             pltpu.VMEM((2, 4, 8, HALF, BLK), jnp.bfloat16),
             pltpu.VMEM((2, 2, 4, 8, HALF, BLK), jnp.bfloat16),
-            pltpu.VMEM((4, 8, ROWS, BLK), jnp.float32),
             pltpu.VMEM((4, 2, 8, HALF, BLK), jnp.bfloat16),
             pltpu.VMEM((2, 4, 8, HALF, BLK), jnp.bfloat16),
             dma((28,)), dma((3,)), dma((3,)), dma((3, 4)), dma((3, 4)), dma((3, NK)), dma((3, NK)),
-            dma((4, 3, 2, 2)), dma((4, 3, 2, 2)), dma((3, 2, 4)), dma((2, 4)), dma((2, 2, 4)), dma((4, 2)), dma((2, 4)),
+            dma((4, 3, 2, 4)), dma((4, 3, 2, 4)), dma((3, 2, 4)), dma((2, 4)), dma((2, 2, 4)), dma((4, 2)), dma((2, 4)),
         ],
         compiler_params=pltpu.CompilerParams(collective_id=0, has_side_effects=True, vmem_limit_bytes=56 * 2**20),
         cost_estimate=pl.CostEstimate(flops=17_200_000_000, bytes_accessed=8_000_000, transcendentals=0),

time: 94.7 us -> 94 us (level)
  Pallas kernels: 92.6 us -> 91.5 us
    pallas_call x1, Pallas kernels: 92.6 us -> 91.5 us  [per_device(): pl.pallas_call(kernel, out_shape=jax.ShapeDtypeStruct((32, 32, BLK), jnp....]
where the time goes in v4:
time: 94 us; the launch traced here: 93.4 us
  Pallas kernels  91.5 us (97%)
  local copies, waits for them, and re-layouts  1.87 us (2%)
    pallas_call x1, Pallas kernels, per_device(): pl.pallas_call(kernel, out_shape=jax.ShapeDtypeStruct((32, 32, BLK), jnp....  91.5 us

profile of v4, /device:TPU:32, one launch (start us, length us, event | category | flops | bytes accessed | tf_op | source)
XLA Modules:
  0.0 93.4 jit_solution(15669298805494104378)
XLA Ops:
  0.0 91.5 %shard_map.73 = bf16[32,32,256]{2,1,0:T(8,128)(2,1)} custom-call(s32[32]{0:T(128)} %lsize.1, s32[16]{0:T(128)} %rsize.1, s32[32]{0:T(128)} %lcharge.1, s32[16]{0:T(128)} %rcharge.1, bf16[2,16,256,256]{3,2,1,0:T(8,128)(2,1)} %psi.1, bf16[8,2,256,256]{3,2,1,0:T(8,128)(2,1)} %left.1, bf16[8,1,256,256]{3,2,1,0:T(8,128)(2,1)} %right.1), custom_call_target="tpu_custom_call" | custom-call | flops 17200001024 | bytes 8000000 | tf_op jit(solution)/shard_map/pallas_call | solution.py:337
  91.5 1.9 %copy.10 = bf16[32,1,32,256]{3,2,1,0:T(8,128)(2,1)} copy(bf16[32,1,32,256]{3,2,1,0:T(8,128)(2,1)} %bitcast.3) | data formatting | bytes 1048576

commit v5 on v4

--- a/solution.py
+++ b/solution.py
@@ -8,8 +8,9 @@
 MESH = pl.DeviceIdType.MESH
 BLK = 256
 NK = 8
-ROWS = 64
-HALF = 32
+BAND = 64
+ROWS = 32
+HALF = 16
 
 
 def wrap(i):
@@ -42,15 +43,16 @@
         pl.semaphore_signal(barrier, 1, device_id=to, device_id_type=MESH)
 
     def start_row(j, half):
-        place = (wrap(x + 2) * ROWS + HALF * half, wrap(x + 1 + 2 * half) * ROWS + HALF * (1 - half), wrap(x + 1 + 2 * half) * ROWS + HALF * half, x * ROWS + HALF * half)[j]
-        return pl.ds(pl.multiple_of(place, HALF), HALF)
+        kind, sub = j // 2, j % 2
+        place = (wrap(x + 2) * BAND + 32 * half, wrap(x + 1 + 2 * half) * BAND + 32 * (1 - half), wrap(x + 1 + 2 * half) * BAND + 32 * half, x * BAND + 32 * half)[kind]
+        return pl.ds(pl.multiple_of(place + HALF * sub, HALF), HALF)
 
     def half_rows(half):
         return pl.ds(HALF * half, HALF)
 
     own = [pltpu.make_async_copy(psi.at[:, sec_at(p, wrap(q + r))], pb.at[r, pl.ds(0, 2)], own_sem.at[r]) for r in range(4)]
     own += [pltpu.make_async_copy(right.at[k, 0], rb.at[0, :, pl.ds(k * BLK, BLK)], own_sem.at[4 + k]) for k in range(NK)]
-    for j in range(4):
+    for j in range(8):
         for a in range(2):
             for h in range(2):
                 own.append(pltpu.make_async_copy(left.at[:, a, start_row(j, h)], lb.at[j, a, :, half_rows(h)], own_sem.at[12 + 4 * j + 2 * a + h]))
@@ -82,7 +84,7 @@
                       l_send.at[j, 0 if to_right else 1, a, h], l_recv.at[j, slot - 1, a, h], dev(dp=1 if to_right else 3))
 
     def l_pass(j, a, piece):
-        pair = pl.ds(2 * piece, 2)
+        pair = pl.ds(4 * piece, 4)
         here = lb.at[j, 2 * (3 if a == 0 else 1) + a, pair]
         return remote(here, lb.at[j, 4 + a, pair], l_send.at[j, 2, a, piece], l_recv.at[j, 1, a, piece], dev(dp=1 if a == 0 else 3))
 
@@ -97,12 +99,12 @@
             for h in range(2):
                 l_copy(j, i, h, True).wait_recv()
             if i == 0:
-                for piece in range(4):
+                for piece in range(2):
                     start(l_pass(j, 0, piece))
             for h in range(2):
                 l_copy(j, 1 - i, h, False).wait_recv()
             if i == 0:
-                for piece in range(4):
+                for piece in range(2):
                     start(l_pass(j, 1, piece))
 
     def px_view(slot_x, piece):
@@ -143,28 +145,32 @@
         power = 1 + 3 * x + lax.div(9 * x * (x - 1), 2) + lax.div(27 * x * (x - 1) * (x - 2), 6)
         return lax.rem(lax.div((212, 49, 171, 78)[n], power), 4)
 
-    def first(j, sectors, begin=0, end=4):
+    def first(j, many, sectors, begin=0, end=4):
         def step(n, _):
             r = wrap(x + slot_order(n))
             for sa in sectors:
-                lhs = lb[j, sa].reshape(NK * ROWS, BLK)
+                lhs = lb[j:j + many, sa].reshape(many * NK * ROWS, BLK)
                 part = jnp.dot(lhs, pm[r, sa], preferred_element_type=jnp.float32).astype(jnp.bfloat16)
-                for k in range(NK):
-                    inner[r, sa * ROWS:(sa + 1) * ROWS, k * BLK:(k + 1) * BLK] = part[k * ROWS:(k + 1) * ROWS]
+                for sub in range(many):
+                    for k in range(NK):
+                        at = (sub * NK + k) * ROWS
+                        inner[r, sub, sa * ROWS:(sa + 1) * ROWS, k * BLK:(k + 1) * BLK] = part[at:at + ROWS]
             return 0
 
         steps = end - begin
-        lax.fori_loop(begin, end, step, 0, unroll=steps if steps < 4 or len(sectors) < 4 else 2)
-
-    def product(r):
-        total = lax.dot_general(inner[r], rb[r], (((1,), (1,)), ((), ())), preferred_element_type=jnp.float32)
-        return total.reshape(8, ROWS, BLK)
-
-    def far_copy(side, r):
-        return remote(stage.at[0, side, r], far.at[side, r], x_send.at[0, side, r], far_recv.at[side, r], dev(dx=(1, 3)[side]))
-
-    def x_copy(j, side, r):
-        return remote(stage.at[j, side, r], near.at[j - 1, side, r], x_send.at[j, side, r], x_recv.at[j - 1, side, r], dev(dx=(1, 3)[side]))
+        lax.fori_loop(begin, end, step, 0, unroll=2 if many == 2 and len(sectors) > 2 else steps)
+
+    def product(r, many):
+        lhs = inner[r, :many].reshape(many * 8 * ROWS, NK * BLK)
+        total = lax.dot_general(lhs, rb[r], (((1,), (1,)), ((), ())), preferred_element_type=jnp.float32)
+        return total.reshape(many, 8, ROWS, BLK)
+
+    def far_copy(sub, side, r):
+        return remote(stage.at[sub, side, r], far.at[sub, side, r], x_send.at[sub, side, r], far_recv.at[sub, side, r], dev(dx=(1, 3)[side]))
+
+    def x_copy(kind, sub, side, r):
+        j = 2 * kind + sub
+        return remote(stage.at[j, side, r], near.at[j - 2, side, r], x_send.at[j, side, r], x_recv.at[j - 2, side, r], dev(dx=(1, 3)[side]))
 
     def fin_copy(r, other):
         core = 1 - c if other else c
@@ -173,49 +179,54 @@
     def halves(total):
         return total[:, :HALF], total[:, HALF:]
 
-    def stage_far(r):
-        for side, part in enumerate(halves(product(r))):
-            stage[0, side, r] = part.astype(jnp.bfloat16)
-            far_copy(side, r).start()
-
-    def stage_one(r):
-        for side, part in enumerate(halves(product(r))):
-            stage[1, side, r] = part.astype(jnp.bfloat16)
-            x_copy(1, side, r).start()
-
-    def stage_two(r):
-        parts = halves(product(r))
-        for side in range(2):
-            far_copy(side, r).wait_recv()
-            stage[2, side, r] = (parts[side] + far[side, r].astype(jnp.float32)).astype(jnp.bfloat16)
-            x_copy(2, side, r).start()
-
-    def stage_own(r):
-        parts = halves(product(r))
-        for h in range(2):
-            x_copy(2 - h, 0, r).wait_recv()
-            x_copy(1 + h, 1, r).wait_recv()
-            total = parts[h] + near[1 - h, 0, r].astype(jnp.float32) + near[h, 1, r].astype(jnp.float32)
-            fin[r, h] = total.astype(jnp.bfloat16)
+    def stage_far(r, sub):
+        for side, part in enumerate(halves(product(r, 1)[0])):
+            stage[sub, side, r] = part.astype(jnp.bfloat16)
+            far_copy(sub, side, r).start()
+
+    def stage_one(r, _):
+        total = product(r, 2)
+        for sub in range(2):
+            for side, part in enumerate(halves(total[sub])):
+                stage[2 + sub, side, r] = part.astype(jnp.bfloat16)
+                x_copy(1, sub, side, r).start()
+
+    def stage_two(r, _):
+        total = product(r, 2)
+        for sub in range(2):
+            for side, part in enumerate(halves(total[sub])):
+                far_copy(sub, side, r).wait_recv()
+                stage[4 + sub, side, r] = (part + far[sub, side, r].astype(jnp.float32)).astype(jnp.bfloat16)
+                x_copy(2, sub, side, r).start()
+
+    def stage_own(r, _):
+        total = product(r, 2)
+        for sub in range(2):
+            for h, part in enumerate(halves(total[sub])):
+                x_copy(2 - h, sub, 0, r).wait_recv()
+                x_copy(1 + h, sub, 1, r).wait_recv()
+                part = part + near[2 * (1 - h) + sub, 0, r].astype(jnp.float32) + near[2 * h + sub, 1, r].astype(jnp.float32)
+                fin[r, h, :, HALF * sub:HALF * (sub + 1)] = part.astype(jnp.bfloat16)
         fin_copy(r, True).start()
 
         @pl.when(r > 0)
         def _():
             fin_copy(r, False).start()
 
-    def run(body, low, high, down=False):
+    def run(body, low, high, sub, down=False):
         def step(n, _):
-            body(3 - n if down else wrap(x + slot_order(n)))
+            r = 3 - n if down else wrap(x + slot_order(n))
+            body(r, sub)
             return 0
 
-        lax.fori_loop(low, high, step, 0, unroll=2 if (high - low) % 2 == 0 else 1)
+        lax.fori_loop(low, high, step, 0, unroll=2)
 
     for s in (1, 3, 2):
         start(p_copy(s))
     for copy in own:
         copy.wait()
     mask_own()
-    first(0, (0, 1))
+    first(0, 1, (0, 1))
     for s in (1, 3):
         p_copy(s).wait_recv()
     for piece in range(2):
@@ -235,6 +246,7 @@
         r_copy(NK - 1 - i, False).wait_recv()
         start(r_pass(NK - 1 - i))
     l_start(0)
+    l_start(1)
     for piece in (0, 1):
         px_arrive(3 - 2 * (piece % 2), piece).wait_recv()
         start(px_pass(piece))
@@ -245,49 +257,71 @@
         r_copy(i, True).wait_recv()
         r_copy(NK - 1 - i, False).wait_recv()
     l_forward(0)
-    l_start(1)
+    l_start(2)
     for piece in range(4):
         px_arrive(1 + 2 * (piece % 2), piece).wait_recv()
     mask_slot(1)
     mask_slot(3)
-    first(0, (2, 3, 6, 7), 0, 3)
-    for piece in range(4):
+    first(0, 1, (2, 3, 6, 7), 0, 3)
+    for piece in range(2):
         l_pass(0, 0, piece).wait_recv()
         l_pass(0, 1, piece).wait_recv()
-    first(0, (4, 5), 0, 3)
+    first(0, 1, (4, 5), 0, 3)
+    l_forward(1)
+    l_start(3)
     for n in (0, 1):
-        stage_far(far_order(n))
+        stage_far(far_order(n), 0)
     for k in range(NK):
         r_pass(k).wait_recv()
-    l_forward(1)
-    l_start(2)
     for piece in range(4):
         px_arrive(2, piece).wait_recv()
     mask_slot(2)
-    first(0, range(2, 8), 3, 4)
+    first(0, 1, range(2, 8), 3, 4)
     for n in (2, 3):
-        stage_far(far_order(n))
-    first(1, (0, 1, 2, 3, 6, 7))
-    for piece in range(4):
+        stage_far(far_order(n), 0)
+    l_forward(2)
+    l_start(4)
+    first(1, 1, (0, 1, 2, 3, 6, 7))
+    for piece in range(2):
         l_pass(1, 0, piece).wait_recv()
         l_pass(1, 1, piece).wait_recv()
-    first(1, (4, 5))
-    l_forward(2)
-    l_start(3)
-    run(stage_one, 0, 4)
-    first(2, (0, 1, 2, 3, 6, 7))
-    for piece in range(4):
+    first(1, 1, (4, 5))
+    l_forward(3)
+    l_start(5)
+    run(stage_far, 0, 4, 1)
+    first(2, 2, (0, 1, 2, 3, 6, 7))
+    for piece in range(2):
         l_pass(2, 0, piece).wait_recv()
         l_pass(2, 1, piece).wait_recv()
-    first(2, (4, 5))
-    l_forward(3)
-    run(stage_two, 0, 4, True)
-    first(3, (0, 1, 2, 3, 6, 7))
-    for piece in range(4):
+    for piece in range(2):
         l_pass(3, 0, piece).wait_recv()
         l_pass(3, 1, piece).wait_recv()
-    first(3, (4, 5))
-    run(stage_own, 0, 4, True)
+    l_forward(4)
+    l_start(6)
+    first(2, 2, (4, 5))
+    run(stage_one, 0, 4, 0)
+    l_forward(5)
+    l_start(7)
+    first(4, 2, (0, 1, 2, 3, 6, 7))
+    for piece in range(2):
+        l_pass(4, 0, piece).wait_recv()
+        l_pass(4, 1, piece).wait_recv()
+    for piece in range(2):
+        l_pass(5, 0, piece).wait_recv()
+        l_pass(5, 1, piece).wait_recv()
+    l_forward(6)
+    first(4, 2, (4, 5))
+    run(stage_two, 0, 4, 0, True)
+    l_forward(7)
+    first(6, 2, (0, 1, 2, 3, 6, 7))
+    for piece in range(2):
+        l_pass(6, 0, piece).wait_recv()
+        l_pass(6, 1, piece).wait_recv()
+    for piece in range(2):
+        l_pass(7, 0, piece).wait_recv()
+        l_pass(7, 1, piece).wait_recv()
+    first(6, 2, (4, 5))
+    run(stage_own, 0, 4, 0, True)
 
     got[c, 0] = fin[0, c]
 
@@ -296,9 +330,10 @@
 
     def drain(r, _):
         for side in range(2):
-            far_copy(side, r).wait_send()
-            x_copy(1, side, r).wait_send()
-            x_copy(2, side, r).wait_send()
+            for sub in range(2):
+                far_copy(sub, side, r).wait_send()
+                x_copy(1, sub, side, r).wait_send()
+                x_copy(2, sub, side, r).wait_send()
         return 0
 
     lax.fori_loop(0, 4, drain, 0)
@@ -322,7 +357,7 @@
         out[a] = jnp.where((row_at < rows) & col_live, total, 0.0).astype(jnp.bfloat16)
         return 0
 
-    lax.fori_loop(0, 32, finish, 0, unroll=4)
+    lax.fori_loop(0, 32, finish, 0)
 
     for r in range(4):
         fin_copy(r, True).wait_send()
@@ -340,18 +375,18 @@
         in_specs=[smem] * 4 + [hbm] * 3,
         out_specs=pl.BlockSpec(memory_space=pltpu.VMEM),
         scratch_shapes=[
-            pltpu.VMEM((4, 8, NK, ROWS, BLK), jnp.bfloat16),
+            pltpu.VMEM((8, 8, NK, ROWS, BLK), jnp.bfloat16),
             pltpu.VMEM((4, BLK, NK * BLK), jnp.bfloat16),
             pltpu.VMEM((4, 8, BLK, BLK), jnp.bfloat16),
             pltpu.VMEM((4, 8, BLK, BLK), jnp.bfloat16),
-            pltpu.VMEM((4, 8 * ROWS, NK * BLK), jnp.bfloat16),
-            pltpu.VMEM((3, 2, 4, 8, HALF, BLK), jnp.bfloat16),
-            pltpu.VMEM((2, 4, 8, HALF, BLK), jnp.bfloat16),
+            pltpu.VMEM((4, 2, 8 * ROWS, NK * BLK), jnp.bfloat16),
+            pltpu.VMEM((6, 2, 4, 8, HALF, BLK), jnp.bfloat16),
             pltpu.VMEM((2, 2, 4, 8, HALF, BLK), jnp.bfloat16),
-            pltpu.VMEM((4, 2, 8, HALF, BLK), jnp.bfloat16),
-            pltpu.VMEM((2, 4, 8, HALF, BLK), jnp.bfloat16),
-            dma((28,)), dma((3,)), dma((3,)), dma((3, 4)), dma((3, 4)), dma((3, NK)), dma((3, NK)),
-            dma((4, 3, 2, 4)), dma((4, 3, 2, 4)), dma((3, 2, 4)), dma((2, 4)), dma((2, 2, 4)), dma((4, 2)), dma((2, 4)),
+            pltpu.VMEM((4, 2, 4, 8, HALF, BLK), jnp.bfloat16),
+            pltpu.VMEM((4, 2, 8, 32, BLK), jnp.bfloat16),
+            pltpu.VMEM((2, 4, 8, 32, BLK), jnp.bfloat16),
+            dma((44,)), dma((3,)), dma((3,)), dma((3, 4)), dma((3, 4)), dma((3, NK)), dma((3, NK)),
+            dma((8, 3, 2, 2)), dma((8, 3, 2, 2)), dma((6, 2, 4)), dma((2, 2, 4)), dma((4, 2, 4)), dma((4, 2)), dma((2, 4)),
         ],
         compiler_params=pltpu.CompilerParams(collective_id=0, has_side_effects=True, vmem_limit_bytes=56 * 2**20),
         cost_estimate=pl.CostEstimate(flops=17_200_000_000, bytes_accessed=8_000_000, transcendentals=0),

time: 94 us -> 93.9 us (level)
  no operation moved by 1% of the time
where the time goes in v5:
time: 93.9 us; the launch traced here: 93.2 us
  Pallas kernels  91.4 us (97%)
  local copies, waits for them, and re-layouts  1.87 us (2%)
    pallas_call x1, Pallas kernels, per_device(): pl.pallas_call(kernel, out_shape=jax.ShapeDtypeStruct((32, 32, BLK), jnp....  91.4 us

profile of v5, /device:TPU:32, one launch (start us, length us, event | category | flops | bytes accessed | tf_op | source)
XLA Modules:
  0.0 93.2 jit_solution(743946347887052071)
XLA Ops:
  0.0 91.4 %shard_map.73 = bf16[32,32,256]{2,1,0:T(8,128)(2,1)} custom-call(s32[32]{0:T(128)} %lsize.1, s32[16]{0:T(128)} %rsize.1, s32[32]{0:T(128)} %lcharge.1, s32[16]{0:T(128)} %rcharge.1, bf16[2,16,256,256]{3,2,1,0:T(8,128)(2,1)} %psi.1, bf16[8,2,256,256]{3,2,1,0:T(8,128)(2,1)} %left.1, bf16[8,1,256,256]{3,2,1,0:T(8,128)(2,1)} %right.1), custom_call_target="tpu_custom_call" | custom-call | flops 17200001024 | bytes 8000000 | tf_op jit(solution)/shard_map/pallas_call | solution.py:372
  91.4 1.9 %copy.10 = bf16[32,1,32,256]{3,2,1,0:T(8,128)(2,1)} copy(bf16[32,1,32,256]{3,2,1,0:T(8,128)(2,1)} %bitcast.3) | data formatting | bytes 1048576
